TPU v7x, 32 devices: a whole 2x2x4 slice. The times are simulated.
32 devices in a mesh: segment: 2 (over x), win: 4 (over y, core), head: 4 (over z).
Axes of the slice: x: 2, y: 2, z: 4, core: 2. Of those that a mesh axis runs over, the one named last changes fastest.
Arguments:
- inputs: bfloat16 [2, 30, 120, 1536], P(None, None, 'win', 'head'), may hold values from -16 to 16
- gains: float32 [2, 1536], P('segment'), may hold values from 0.1 to 1.9
- qkv_weight: bfloat16 [2, 1536, 3, 1536], P('segment', None, None, 'head'), may hold values from -3.5 to 3.5
- out_weight: bfloat16 [2, 1536, 1536], P('segment', 'head'), may hold values from -0.15625 to 0.15625
- labels: int32 [30, 120], P(None, 'win'), may hold values from 0 to 3, as said below
Outputs:
- sections: bfloat16 [2, 2, 30, 120, 1536], P('segment', None, None, 'win', 'head')
Inputs may be any that keep to these rules, and one draw needn't show every extreme that they name: In each window of 30 by 30 cells the label is 2 on the rows from a drawn row cut on plus 1 on the columns from a drawn column cut on; both cuts lie in 1 to 29, so every window holds all four labels.
All inputs are finite; a program needn't handle non-finite values.
Results may differ from a plain program's by a relative error of at most 0.013.
Values may be sent and summed in bfloat16 or wider, within the bound.
A program may use at most 128 MiB of HBM per device.

v0:
```python
import jax
import jax.numpy as jnp
from jax import lax
from jax.sharding import PartitionSpec as P

HEAD_DIM = 128
WIN_SIDE = 30


def passed_along(array, axis, by):
    length = lax.axis_size(axis)
    return lax.ppermute(array, axis, [(i, (i + by) % length) for i in range(length)])


def shifted(value, axis, steps):
    count = lax.axis_size(axis)
    first, last = (max(0, -steps), min(count, count - steps))
    return lax.ppermute(value, axis, [(source, source + steps) for source in range(first, last)])


def rms_normed(slab, gain_row):
    values_f = slab.astype(jnp.float32)
    mean_square = jnp.mean(values_f * values_f, axis=-1, keepdims=True)
    return (values_f * lax.rsqrt(mean_square + 1e-05) * gain_row).astype(jnp.bfloat16)


def to_windows(grid):
    win_rows = grid.shape[0]
    win_count = grid.shape[1] // win_rows
    features = grid.shape[2]
    return (
        grid.reshape(win_rows, win_count, win_rows, features)
        .transpose(1, 0, 2, 3)
        .reshape(win_count, win_rows * win_rows, features)
    )


def from_windows(blocks, win_rows):
    win_count = blocks.shape[0]
    features = blocks.shape[2]
    return (
        blocks.reshape(win_count, win_rows, win_rows, features)
        .transpose(1, 0, 2, 3)
        .reshape(win_rows, win_count * win_rows, features)
    )


def window_layer(current, gain_row, qkv_local, allowed, project):
    gathered = lax.all_gather(current, "head", axis=2, tiled=True)
    normed = rms_normed(gathered, gain_row)
    win_normed = to_windows(normed)
    projected_qkv = jnp.einsum(
        "wtd,dcf->wtcf", win_normed, qkv_local, preferred_element_type=jnp.float32
    ).astype(jnp.bfloat16)
    win_count = projected_qkv.shape[0]
    tokens = projected_qkv.shape[1]
    local_feat = projected_qkv.shape[3]
    heads_local = local_feat // HEAD_DIM
    split_qkv = projected_qkv.reshape(win_count, tokens, 3, heads_local, HEAD_DIM)
    queries = split_qkv[:, :, 0]
    keys_all = split_qkv[:, :, 1]
    values_all = split_qkv[:, :, 2]
    scores = jnp.einsum(
        "wqhe,wkhe->whqk", queries, keys_all, preferred_element_type=jnp.float32
    ) * HEAD_DIM ** (-0.5)
    scores = jnp.where(allowed[:, None], scores, -1e30)
    top_score = jnp.max(scores, axis=-1, keepdims=True)
    expo = jnp.exp(scores - top_score)
    attn_prob = (expo / jnp.sum(expo, axis=-1, keepdims=True)).astype(jnp.bfloat16)
    attended = jnp.einsum(
        "whqk,wkhe->wqhe", attn_prob, values_all, preferred_element_type=jnp.float32
    ).astype(jnp.bfloat16)
    attended = attended.reshape(win_count, tokens, local_feat)
    grid_att = from_windows(attended, current.shape[0])
    projected = project(grid_att)
    return (current.astype(jnp.float32) + projected).astype(jnp.bfloat16)


def body(inputs, gains, qkv_weight, out_weight, labels):
    segment_id = lax.axis_index("segment")
    micro_count = inputs.shape[0]
    gain_row = gains[0]
    qkv_local = qkv_weight[0]
    out_local = out_weight[0]
    win_labels = to_windows(labels[:, :, None])[:, :, 0]
    allowed = (win_labels[:, :, None] == win_labels[:, None, :]) | (segment_id == 0)
    half_cols = WIN_SIDE // 2
    w_columns = lax.all_to_all(out_local, "head", split_axis=1, concat_axis=0, tiled=True)

    def project(grid_att):
        return jnp.einsum(
            "rcf,fg->rcg",
            lax.all_gather(grid_att, "head", axis=2, tiled=True),
            w_columns,
            preferred_element_type=jnp.float32,
        )

    def advance(incoming, step_id):
        fresh = lax.dynamic_index_in_dim(
            inputs, jnp.minimum(step_id, micro_count - 1), 0, keepdims=False
        )
        current = jnp.where(segment_id == 0, fresh, incoming)
        leading = passed_along(current[:, :half_cols], "win", -1)
        rolled = jnp.concatenate([current[:, half_cols:], leading], axis=1)
        current = jnp.where(segment_id == 1, rolled, current)
        result = window_layer(current, gain_row, qkv_local, allowed, project)
        passed = shifted(result, "segment", 1)
        return (passed, result)

    start_slab = jnp.zeros(inputs.shape[1:], jnp.bfloat16)
    _, produced = lax.scan(advance, start_slab, jnp.arange(micro_count + 1, dtype=jnp.int32))
    sections = lax.dynamic_slice_in_dim(produced, segment_id, micro_count, 0)
    return sections[None]


def solution(mesh):
    in_specs = (
        P(None, None, "win", "head"),
        P("segment", None),
        P("segment", None, None, "head"),
        P("segment", "head", None),
        P(None, "win"),
    )
    out_specs = P("segment", None, None, "win", "head")
    return jax.shard_map(body, mesh=mesh, in_specs=in_specs, out_specs=out_specs, check_vma=False)
```

profile of v0, /device:TPU:0, one launch (start us, length us, event | category | flops | bytes accessed | tf_op | source)
XLA Modules:
  0.0 605.7 jit_solution(16720629512955874780)
XLA Ops:
  6.5 2.5 all_to_all.14
  10.2 6.4 %all-to-all-start = ((bf16[384,4,384]{2,0,1:T(8,128)(2,1)}), bf16[384,4,384]{2,0,1:T(8,128)(2,1)}, u32[]{:S(2)}, u32[]{:S(2)}) async-start(bf16[384,4,384]{2,0,1:T(8,128)(2,1)} %copy.19), calls=%async_computation | async-start | bytes 2359296 | tf_op jit(solution)/shard_map/all_to_all | solution.py:88
  17.0 28.3 %all-to-all-done = bf16[384,4,384]{2,0,1:T(8,128)(2,1)} async-done(((bf16[384,4,384]{2,0,1:T(8,128)(2,1)}), bf16[384,4,384]{2,0,1:T(8,128)(2,1)}, u32[]{:S(2)}, u32[]{:S(2)}) %all-to-all-start) | async-done | bytes 1179680 | tf_op jit(solution)/shard_map/all_to_all | solution.py:88
  45.4 549.4 %while.16 = (s32[]{:T(128)}, bf16[30,30,384]{2,1,0:T(8,128)(2,1)S(1)}, bf16[3,30,30,384]{3,2,1,0:T(8,128)(2,1)}, pred[]{:T(512)}, pred[]{:T(512)}, /*index=5*/s3...) while((s32[]{:T(128)}, ...), condition=%wide.region_4.5_spmd.clone.clone, body=%wide.region_0.4_spmd.clone.clone.sunk | while | flops 5521264128 | bytes 118649424 | solution.py:111
  47.3 5.0 collective-permute-done
  53.7 1.6 or_bitcast_fusion.2
  55.3 57.9 %all-gather.3.cloned.1.call-done = bf16[30,30,1536]{2,1,0:T(8,128)(2,1)} async-done(((bf16[30,30,384]{2,1,0:T(8,128)(2,1)}), bf16[30,30,1536]{2,1,0:T(8,128)(2,1)}) %all-gather.3.cloned.1.call-update) | async-done | bytes 2764816 | tf_op jit(solution)/shard_map/while/body/eval_jaxpr/all_gather | solution.py:49
  113.2 2.7 fusion.39
  116.7 2.2 reshape.166
  118.9 7.9 %convolution_convert_fusion.2 = bf16[900,3,384]{2,0,1:T(8,128)(2,1)} fusion(bf16[900,1536,1]{1,0,2:T(8,128)(2,1)} %reshape.166, bf16[1536,3,384]{2,0,1:T(8,128)(2,1)} %get-tuple-element.350), kind=kOutput, calls=%fused_computation.16.clone.1 | convolution fusion | flops 3186086400 | bytes 8377344 | tf_op jit(solution)/shard_map/while/body/eval_jaxpr/wtd,dcf->wtcf/dot_general | solution.py:52
  126.9 2.9 copy.30
  129.7 7.3 %fusion.41 = (f32[3,900]{1,0:T(4,128)S(1)}, f32[3,900,900]{1,2,0:T(8,128)}) fusion(pred[900,900]{0,1:T(8,128)(4,1)S(1)} %copy-done.2, bf16[1,900,3,3,128]{1,4,3,2,0:T(8,128)(2,1)S(1)} %bitcast.83), kind=kOutput, calls=%fused_computation.36.clone.1 | convolution fusion | flops 631800960 | bytes 12229360 | tf_op jit(solution)/shard_map/while/body/eval_jaxpr/sub | solution.py:68
  137.1 6.4 %fusion.42 = bf16[1,900,3,128]{3,1,2,0:T(8,128)(2,1)S(1)} fusion(f32[3,900,900]{1,2,0:T(8,128)} %get-tuple-element.306, f32[3,900]{1,0:T(4,128)S(1)} %get-tuple-element.307, bf16[1,900,3,3,128]{1,4,3,2,0:T(8,128)(2,1)S(1)} %bitcast.84), kind=kOutput, calls=%fused_computation.19.clone.1 | convolution fusion | flops 627285632 | bytes 11214016 | tf_op jit(solution)/shard_map/while/body/eval_jaxpr/whqk,wkhe->wqhe/dot_general | solution.py:70
  143.8 1.4 reshape.167
  145.2 58.8 %all-gather.5.cloned.1.call-done = bf16[30,30,1536]{2,1,0:T(8,128)(2,1)} async-done(((bf16[30,30,384]{2,1,0:T(8,128)(2,1)}), bf16[30,30,1536]{2,1,0:T(8,128)(2,1)}) %all-gather.5.cloned.1.call-update) | async-done | bytes 2764816 | tf_op jit(solution)/shard_map/while/body/eval_jaxpr/all_gather | solution.py:93
  204.0 4.8 bitcast_dynamic-update-slice_fusion.2
  208.8 3.4 collective-permute-start.1
  212.3 15.6 %collective-permute-done.1 = bf16[30,30,384]{2,1,0:T(8,128)(2,1)S(1)} collective-permute-done((bf16[30,30,384]{2,1,0:T(8,128)(2,1)S(1)}, bf16[30,30,384]{2,1,0:T(8,128)(2,1)S(1)}, u32[]{:S(2)}, u32[]{:S(2)}) %collective-permute-start.1) | collective-permute-done | bytes 691232 | tf_op jit(solution)/shard_map/while/body/eval_jaxpr/ppermute | solution.py:18
  229.5 5.0 collective-permute-done
  235.9 1.6 or_bitcast_fusion.2
  237.5 59.1 %all-gather.3.cloned.1.call-done = bf16[30,30,1536]{2,1,0:T(8,128)(2,1)} async-done(((bf16[30,30,384]{2,1,0:T(8,128)(2,1)}), bf16[30,30,1536]{2,1,0:T(8,128)(2,1)}) %all-gather.3.cloned.1.call-update) | async-done | bytes 2764816 | tf_op jit(solution)/shard_map/while/body/eval_jaxpr/all_gather | solution.py:49
  296.6 2.7 fusion.39
  300.1 2.2 reshape.166
  302.3 7.9 %convolution_convert_fusion.2 = bf16[900,3,384]{2,0,1:T(8,128)(2,1)} fusion(bf16[900,1536,1]{1,0,2:T(8,128)(2,1)} %reshape.166, bf16[1536,3,384]{2,0,1:T(8,128)(2,1)} %get-tuple-element.350), kind=kOutput, calls=%fused_computation.16.clone.1 | convolution fusion | flops 3186086400 | bytes 8377344 | tf_op jit(solution)/shard_map/while/body/eval_jaxpr/wtd,dcf->wtcf/dot_general | solution.py:52
  310.3 2.9 copy.30
  313.1 7.3 %fusion.41 = (f32[3,900]{1,0:T(4,128)S(1)}, f32[3,900,900]{1,2,0:T(8,128)}) fusion(pred[900,900]{0,1:T(8,128)(4,1)S(1)} %copy-done.2, bf16[1,900,3,3,128]{1,4,3,2,0:T(8,128)(2,1)S(1)} %bitcast.83), kind=kOutput, calls=%fused_computation.36.clone.1 | convolution fusion | flops 631800960 | bytes 12229360 | tf_op jit(solution)/shard_map/while/body/eval_jaxpr/sub | solution.py:68
  320.5 6.4 %fusion.42 = bf16[1,900,3,128]{3,1,2,0:T(8,128)(2,1)S(1)} fusion(f32[3,900,900]{1,2,0:T(8,128)} %get-tuple-element.306, f32[3,900]{1,0:T(4,128)S(1)} %get-tuple-element.307, bf16[1,900,3,3,128]{1,4,3,2,0:T(8,128)(2,1)S(1)} %bitcast.84), kind=kOutput, calls=%fused_computation.19.clone.1 | convolution fusion | flops 627285632 | bytes 11214016 | tf_op jit(solution)/shard_map/while/body/eval_jaxpr/whqk,wkhe->wqhe/dot_general | solution.py:70
  327.2 1.4 reshape.167
  328.6 58.8 %all-gather.5.cloned.1.call-done = bf16[30,30,1536]{2,1,0:T(8,128)(2,1)} async-done(((bf16[30,30,384]{2,1,0:T(8,128)(2,1)}), bf16[30,30,1536]{2,1,0:T(8,128)(2,1)}) %all-gather.5.cloned.1.call-update) | async-done | bytes 2764816 | tf_op jit(solution)/shard_map/while/body/eval_jaxpr/all_gather | solution.py:93
  387.4 4.9 bitcast_dynamic-update-slice_fusion.2
  392.3 3.4 collective-permute-start.1
  395.7 15.6 %collective-permute-done.1 = bf16[30,30,384]{2,1,0:T(8,128)(2,1)S(1)} collective-permute-done((bf16[30,30,384]{2,1,0:T(8,128)(2,1)S(1)}, bf16[30,30,384]{2,1,0:T(8,128)(2,1)S(1)}, u32[]{:S(2)}, u32[]{:S(2)}) %collective-permute-start.1) | collective-permute-done | bytes 691232 | tf_op jit(solution)/shard_map/while/body/eval_jaxpr/ppermute | solution.py:18
  413.0 5.0 collective-permute-done
  419.3 1.6 or_bitcast_fusion.2
  420.9 59.1 %all-gather.3.cloned.1.call-done = bf16[30,30,1536]{2,1,0:T(8,128)(2,1)} async-done(((bf16[30,30,384]{2,1,0:T(8,128)(2,1)}), bf16[30,30,1536]{2,1,0:T(8,128)(2,1)}) %all-gather.3.cloned.1.call-update) | async-done | bytes 2764816 | tf_op jit(solution)/shard_map/while/body/eval_jaxpr/all_gather | solution.py:49
  480.0 2.7 fusion.39
  483.5 2.2 reshape.166
  485.7 7.9 %convolution_convert_fusion.2 = bf16[900,3,384]{2,0,1:T(8,128)(2,1)} fusion(bf16[900,1536,1]{1,0,2:T(8,128)(2,1)} %reshape.166, bf16[1536,3,384]{2,0,1:T(8,128)(2,1)} %get-tuple-element.350), kind=kOutput, calls=%fused_computation.16.clone.1 | convolution fusion | flops 3186086400 | bytes 8377344 | tf_op jit(solution)/shard_map/while/body/eval_jaxpr/wtd,dcf->wtcf/dot_general | solution.py:52
  493.7 2.9 copy.30
  496.6 7.3 %fusion.41 = (f32[3,900]{1,0:T(4,128)S(1)}, f32[3,900,900]{1,2,0:T(8,128)}) fusion(pred[900,900]{0,1:T(8,128)(4,1)S(1)} %copy-done.2, bf16[1,900,3,3,128]{1,4,3,2,0:T(8,128)(2,1)S(1)} %bitcast.83), kind=kOutput, calls=%fused_computation.36.clone.1 | convolution fusion | flops 631800960 | bytes 12229360 | tf_op jit(solution)/shard_map/while/body/eval_jaxpr/sub | solution.py:68
  503.9 6.4 %fusion.42 = bf16[1,900,3,128]{3,1,2,0:T(8,128)(2,1)S(1)} fusion(f32[3,900,900]{1,2,0:T(8,128)} %get-tuple-element.306, f32[3,900]{1,0:T(4,128)S(1)} %get-tuple-element.307, bf16[1,900,3,3,128]{1,4,3,2,0:T(8,128)(2,1)S(1)} %bitcast.84), kind=kOutput, calls=%fused_computation.19.clone.1 | convolution fusion | flops 627285632 | bytes 11214016 | tf_op jit(solution)/shard_map/while/body/eval_jaxpr/whqk,wkhe->wqhe/dot_general | solution.py:70
  510.6 1.4 reshape.167
  512.0 58.8 %all-gather.5.cloned.1.call-done = bf16[30,30,1536]{2,1,0:T(8,128)(2,1)} async-done(((bf16[30,30,384]{2,1,0:T(8,128)(2,1)}), bf16[30,30,1536]{2,1,0:T(8,128)(2,1)}) %all-gather.5.cloned.1.call-update) | async-done | bytes 2764816 | tf_op jit(solution)/shard_map/while/body/eval_jaxpr/all_gather | solution.py:93
  570.9 4.9 bitcast_dynamic-update-slice_fusion.2
  575.7 3.4 collective-permute-start.1
  579.2 15.6 %collective-permute-done.1 = bf16[30,30,384]{2,1,0:T(8,128)(2,1)S(1)} collective-permute-done((bf16[30,30,384]{2,1,0:T(8,128)(2,1)S(1)}, bf16[30,30,384]{2,1,0:T(8,128)(2,1)S(1)}, u32[]{:S(2)}, u32[]{:S(2)}) %collective-permute-start.1) | collective-permute-done | bytes 691232 | tf_op jit(solution)/shard_map/while/body/eval_jaxpr/ppermute | solution.py:18
  594.8 1.5 constant_dynamic-slice_fusion
  596.3 2.5 copy.27
  (81 shorter events, 12.1 us)
Async XLA Ops:
  9.1 7.6 %copy-start.5 = (bf16[2,30,30,384]{3,0,2,1:T(2,128)(2,1)S(1)}, bf16[2,30,30,384]{3,0,2,1:T(2,128)(2,1)}, u32[]{:S(2)}) copy-start(bf16[2,30,30,384]{3,0,2,1:T(2,128)(2,1)} %param.7) | copy-start | bytes 4147204
  10.2 6.7 %copy-start.7 = (s32[30,30]{1,0:T(8,128)S(1)}, s32[30,30]{1,0:T(8,128)}, u32[]{:S(2)}) copy-start(s32[30,30]{1,0:T(8,128)} %param.11) | copy-start | bytes 10804
  10.2 35.2 %copy-start.6 = (f32[1,1536]{1,0:T(1,128)S(1)}, f32[1,1536]{1,0:T(1,128)}, u32[]{:S(2)}) copy-start(f32[1,1536]{1,0:T(1,128)} %param.8) | copy-start | bytes 18436
  10.2 35.1 %all-to-all-start = ((bf16[384,4,384]{2,0,1:T(8,128)(2,1)}), bf16[384,4,384]{2,0,1:T(8,128)(2,1)}, u32[]{:S(2)}, u32[]{:S(2)}) async-start(bf16[384,4,384]{2,0,1:T(8,128)(2,1)} %copy.19), calls=%async_computation | async-start | bytes 2359296 | tf_op jit(solution)/shard_map/all_to_all | solution.py:88
  45.4 8.2 %copy-start.3 = (bf16[2,30,30,384]{3,2,1,0:T(8,128)(2,1)}, bf16[2,30,30,384]{3,2,1,0:T(8,128)(2,1)S(1)}, u32[]{:S(2)}) copy-start(bf16[2,30,30,384]{3,2,1,0:T(8,128)(2,1)S(1)} %get-tuple-element.348) | copy-start | bytes 4147204 | tf_op jit(solution)/shard_map/while
  45.4 67.8 %all-gather.3.cloned.1.call-start = ((), (), s32[]{:S(2)}) async-start(), calls=%async_computation.1 | async-start | bytes 3686400 | tf_op jit(solution)/shard_map/while/body/eval_jaxpr/all_gather | solution.py:49
  47.1 5.3 collective-permute-start
  53.6 150.4 %all-gather.5.cloned.1.call-start = ((), (), s32[]{:S(2)}) async-start(), calls=%async_computation.2 | async-start | bytes 3686400 | tf_op jit(solution)/shard_map/while/body/eval_jaxpr/all_gather | solution.py:93
  113.2 2.7 copy-start
  126.9 2.9 copy-start.2
  143.4 60.6 %copy-start.1 = (bf16[30,30,384]{2,1,0:T(8,128)(2,1)S(1)}, bf16[30,30,384]{2,1,0:T(8,128)(2,1)}, u32[]{:S(2)}) copy-start(bf16[30,30,384]{2,1,0:T(8,128)(2,1)} %maximum_select_fusion.2) | copy-start | bytes 2073604 | tf_op jit(solution)/shard_map/while
  204.0 23.9 %copy-start.4 = (bf16[2,30,30,384]{3,2,1,0:T(8,128)(2,1)S(1)}, bf16[2,30,30,384]{3,2,1,0:T(8,128)(2,1)}, u32[]{:S(2)}) copy-start(bf16[2,30,30,384]{3,2,1,0:T(8,128)(2,1)} %copy-done.3) | copy-start | bytes 4147204 | tf_op jit(solution)/shard_map/while
  208.8 19.1 %collective-permute-start.1 = (bf16[30,30,384]{2,1,0:T(8,128)(2,1)S(1)}, bf16[30,30,384]{2,1,0:T(8,128)(2,1)S(1)}, u32[]{:S(2)}, u32[]{:S(2)}) collective-permute-start(bf16[30,30,384]{2,1,0:T(8,128)(2,1)S(1)} %get-tuple-element.308), channel_id=1, source_target_pairs={{0,16},{1,17},{2,18},{3,19},{4,20},{5,21},{6,22},{7,23},{8,24},{9,... | collective-permute-start | bytes 2073608 | tf_op jit(solution)/shard_map/while/body/eval_jaxpr/ppermute | solution.py:18
  227.9 7.9 %copy-start.3 = (bf16[2,30,30,384]{3,2,1,0:T(8,128)(2,1)}, bf16[2,30,30,384]{3,2,1,0:T(8,128)(2,1)S(1)}, u32[]{:S(2)}) copy-start(bf16[2,30,30,384]{3,2,1,0:T(8,128)(2,1)S(1)} %get-tuple-element.348) | copy-start | bytes 4147204 | tf_op jit(solution)/shard_map/while
  227.9 68.7 %all-gather.3.cloned.1.call-start = ((), (), s32[]{:S(2)}) async-start(), calls=%async_computation.1 | async-start | bytes 3686400 | tf_op jit(solution)/shard_map/while/body/eval_jaxpr/all_gather | solution.py:49
  229.5 5.1 collective-permute-start
  235.8 151.6 %all-gather.5.cloned.1.call-start = ((), (), s32[]{:S(2)}) async-start(), calls=%async_computation.2 | async-start | bytes 3686400 | tf_op jit(solution)/shard_map/while/body/eval_jaxpr/all_gather | solution.py:93
  296.6 2.7 copy-start
  310.3 2.9 copy-start.2
  326.8 60.6 %copy-start.1 = (bf16[30,30,384]{2,1,0:T(8,128)(2,1)S(1)}, bf16[30,30,384]{2,1,0:T(8,128)(2,1)}, u32[]{:S(2)}) copy-start(bf16[30,30,384]{2,1,0:T(8,128)(2,1)} %maximum_select_fusion.2) | copy-start | bytes 2073604 | tf_op jit(solution)/shard_map/while
  387.4 23.9 %copy-start.4 = (bf16[2,30,30,384]{3,2,1,0:T(8,128)(2,1)S(1)}, bf16[2,30,30,384]{3,2,1,0:T(8,128)(2,1)}, u32[]{:S(2)}) copy-start(bf16[2,30,30,384]{3,2,1,0:T(8,128)(2,1)} %copy-done.3) | copy-start | bytes 4147204 | tf_op jit(solution)/shard_map/while
  392.3 19.1 %collective-permute-start.1 = (bf16[30,30,384]{2,1,0:T(8,128)(2,1)S(1)}, bf16[30,30,384]{2,1,0:T(8,128)(2,1)S(1)}, u32[]{:S(2)}, u32[]{:S(2)}) collective-permute-start(bf16[30,30,384]{2,1,0:T(8,128)(2,1)S(1)} %get-tuple-element.308), channel_id=1, source_target_pairs={{0,16},{1,17},{2,18},{3,19},{4,20},{5,21},{6,22},{7,23},{8,24},{9,... | collective-permute-start | bytes 2073608 | tf_op jit(solution)/shard_map/while/body/eval_jaxpr/ppermute | solution.py:18
  411.3 7.9 %copy-start.3 = (bf16[2,30,30,384]{3,2,1,0:T(8,128)(2,1)}, bf16[2,30,30,384]{3,2,1,0:T(8,128)(2,1)S(1)}, u32[]{:S(2)}) copy-start(bf16[2,30,30,384]{3,2,1,0:T(8,128)(2,1)S(1)} %get-tuple-element.348) | copy-start | bytes 4147204 | tf_op jit(solution)/shard_map/while
  411.3 68.7 %all-gather.3.cloned.1.call-start = ((), (), s32[]{:S(2)}) async-start(), calls=%async_computation.1 | async-start | bytes 3686400 | tf_op jit(solution)/shard_map/while/body/eval_jaxpr/all_gather | solution.py:49
  412.9 5.1 collective-permute-start
  419.2 151.6 %all-gather.5.cloned.1.call-start = ((), (), s32[]{:S(2)}) async-start(), calls=%async_computation.2 | async-start | bytes 3686400 | tf_op jit(solution)/shard_map/while/body/eval_jaxpr/all_gather | solution.py:93
  480.0 2.7 copy-start
  493.7 2.9 copy-start.2
  510.3 60.6 %copy-start.1 = (bf16[30,30,384]{2,1,0:T(8,128)(2,1)S(1)}, bf16[30,30,384]{2,1,0:T(8,128)(2,1)}, u32[]{:S(2)}) copy-start(bf16[30,30,384]{2,1,0:T(8,128)(2,1)} %maximum_select_fusion.2) | copy-start | bytes 2073604 | tf_op jit(solution)/shard_map/while
  570.9 24.0 %copy-start.4 = (bf16[2,30,30,384]{3,2,1,0:T(8,128)(2,1)S(1)}, bf16[2,30,30,384]{3,2,1,0:T(8,128)(2,1)}, u32[]{:S(2)}) copy-start(bf16[2,30,30,384]{3,2,1,0:T(8,128)(2,1)} %copy-done.3) | copy-start | bytes 4147204 | tf_op jit(solution)/shard_map/while
  575.7 19.1 %collective-permute-start.1 = (bf16[30,30,384]{2,1,0:T(8,128)(2,1)S(1)}, bf16[30,30,384]{2,1,0:T(8,128)(2,1)S(1)}, u32[]{:S(2)}, u32[]{:S(2)}) collective-permute-start(bf16[30,30,384]{2,1,0:T(8,128)(2,1)S(1)} %get-tuple-element.308), channel_id=1, source_target_pairs={{0,16},{1,17},{2,18},{3,19},{4,20},{5,21},{6,22},{7,23},{8,24},{9,... | collective-permute-start | bytes 2073608 | tf_op jit(solution)/shard_map/while/body/eval_jaxpr/ppermute | solution.py:18
Sparse Core Ops, SparseCore 0:
  53.7 59.4 all-gather.2
  145.3 58.6 all-gather.4
  235.9 60.6 all-gather.2
  328.7 58.6 all-gather.4
  419.4 60.6 all-gather.2
  512.1 58.6 all-gather.4
where the time goes:
time: 606 us
  waiting for transfers between devices  443 us (73%)
  matrix products  79.5 us (13%)
  local copies, waits for them, and re-layouts  31.2 us (5%)
  other arithmetic  19 us (3%)
  starting transfers between devices  17.2 us (3%)
  between operations  13.4 us (2%)
    all_gather x3, waiting for transfers between devices, project(): lax.all_gather(grid_att, 'head', axis=2, tiled=True)  176 us
    all_gather x3, waiting for transfers between devices, window_layer(): gathered = lax.all_gather(current, 'head', axis=2, tiled=True)  176 us
    ppermute x3, waiting for transfers between devices, shifted(): lax.ppermute(value, axis, [(source, source + steps) for source in range(f...  46.9 us
    all_to_all x1, waiting for transfers between devices, body(): lax.all_to_all(out_local, 'head', split_axis=1, concat_axis=0, tiled=True)  28.3 us
    dot_general x3, matrix products, window_layer(): jnp.einsum('wtd,dcf->wtcf', win_normed, qkv_local, preferred_element_type...  23.8 us
    sub x3, matrix products, window_layer(): expo = jnp.exp(scores - top_score)  22 us
    dot_general x3, matrix products, window_layer(): jnp.einsum('whqk,wkhe->wqhe', attn_prob, values_all, preferred_element_ty...  19.1 us
    ppermute x3, waiting for transfers between devices, passed_along(): lax.ppermute(array, axis, [(i, (i + by) % length) for i in range(length)])  15.1 us
  transfers between devices with their start and end apart: 13, of which 13 were waited for; matrix products, arithmetic and copies ran while one was open for 1% of the time, Pallas kernels for 0%

commit v1 on v0

v1 whole, which is shorter than its diff:
```python
import functools
import math

import jax
import jax.numpy as jnp
from jax import lax
from jax.experimental import pallas as pl
from jax.experimental.pallas import tpu as pltpu
from jax.sharding import PartitionSpec as P

HEAD_DIM = 128
WIN_SIDE = 30
MESH = pl.DeviceIdType.MESH
LAYERS = 2


def pad16(n):
    return -(-n // 16) * 16


def remote(src, dst, send, recv, device):
    return pltpu.make_async_remote_copy(
        src_ref=src, dst_ref=dst, send_sem=send, recv_sem=recv,
        device_id=device, device_id_type=MESH,
    )


def two_layers(
    n_head, n_win, half,
    x_ref, gain_ref, lq_ref, lk_ref, wq_hbm, wo_hbm,
    out_ref,
    wq, wo, gb, ag, normed, qkv, vx, attb, part, parts_in, own, cur, first_a, second,
    loc_sem, wsend, wrecv, fsend, frecv, ag_send, ag_recv, rs_send, rs_recv,
    roll_send, roll_recv, o_send, o_recv,
):
    seg = lax.axis_index("segment")
    win = lax.axis_index("win")
    me = lax.axis_index("head")
    other = 1 - seg
    core = lax.rem(win, 2)
    mate = win + 1 - 2 * core
    left = lax.rem(win + n_win - 1, n_win)
    right = lax.rem(win + 1, n_win)
    peers = [lax.rem(me + d, n_head) for d in range(1, n_head)]
    tokens, feat = x_ref.shape
    heads = feat // HEAD_DIM
    first_rows = pad16(half // 2)
    subs = ((0, first_rows), (first_rows, half - first_rows))

    barrier = pltpu.get_barrier_semaphore()
    for peer in peers:
        pl.semaphore_signal(barrier, inc=1, device_id={"head": peer}, device_id_type=MESH)
    pl.semaphore_signal(barrier, inc=1, device_id={"segment": other}, device_id_type=MESH)
    for w in (mate, left, right):
        pl.semaphore_signal(barrier, inc=1, device_id={"win": w}, device_id_type=MESH)

    wq_local = pltpu.make_async_copy(wq_hbm, wq.at[seg], loc_sem.at[0])
    wo_local = pltpu.make_async_copy(wo_hbm, wo.at[seg], loc_sem.at[1])
    wq_local.start()
    wo_local.start()
    pl.semaphore_wait(barrier, n_head - 1 + 4)

    def gather_copies(layer, h, src):
        rows = pl.ds(h * half, half)
        return [
            remote(src.at[rows], ag.at[layer, d, rows], ag_send.at[layer, h, d],
                   ag_recv.at[layer, h, d], {"head": peers[d]})
            for d in range(n_head - 1)
        ]

    gathers = [[None, None], [None, None]]
    for h in range(2):
        gathers[0][h] = gather_copies(0, h, x_ref)
        for c in gathers[0][h]:
            c.start()

    q_rows, o_rows = wq_hbm.shape[0] // 2, wo_hbm.shape[0] // 2
    mine_q = pl.ds(pl.multiple_of(core * q_rows, 16), q_rows)
    mine_o = pl.ds(pl.multiple_of(core * o_rows, 16), o_rows)
    mate_q = pl.ds(pl.multiple_of((1 - core) * q_rows, 16), q_rows)
    mate_o = pl.ds(pl.multiple_of((1 - core) * o_rows, 16), o_rows)
    there, beside = {"segment": other}, {"win": mate}
    gain_out = remote(gain_ref, gb.at[seg], wsend.at[2], wrecv.at[2], there)
    wq_out = remote(wq_hbm.at[mine_q], wq.at[seg, mine_q], wsend.at[0], wrecv.at[0], there)
    wo_out = remote(wo_hbm.at[mine_o], wo.at[seg, mine_o], wsend.at[1], wrecv.at[1], there)
    gain_out.start()
    wq_out.start()
    wo_out.start()
    gb[seg] = gain_ref[...]
    for h in range(heads):
        vx[h, :, HEAD_DIM:] = jnp.ones((tokens, HEAD_DIM), jnp.bfloat16)

    wq_in = remote(wq_hbm.at[mine_q], wq.at[other, mine_q], wsend.at[0], wrecv.at[0], there)
    wo_in = remote(wo_hbm.at[mine_o], wo.at[other, mine_o], wsend.at[1], wrecv.at[1], there)
    gain_in = remote(gain_ref, gb.at[other], wsend.at[2], wrecv.at[2], there)
    wq_fwd = remote(wq.at[other, mine_q], wq.at[other, mine_q], fsend.at[0], frecv.at[0], beside)
    wo_fwd = remote(wo.at[other, mine_o], wo.at[other, mine_o], fsend.at[1], frecv.at[1], beside)
    wq_fwd_in = remote(wq.at[other, mate_q], wq.at[other, mate_q], fsend.at[0], frecv.at[0], beside)
    wo_fwd_in = remote(wo.at[other, mate_o], wo.at[other, mate_o], fsend.at[1], frecv.at[1], beside)

    def part_copy(layer, block, rows, d):
        return remote(part.at[layer, d, rows], parts_in.at[layer, d, rows],
                      rs_send.at[layer, block, d], rs_recv.at[layer, block, d],
                      {"head": peers[d]})

    def columns(owner):
        return pl.ds(pl.multiple_of(owner * feat, 128), feat)

    def layer_compute(layer, src):
        for h in range(2):
            for c in gathers[layer][h]:
                c.wait_recv()

        def norm_half(i, carry):
            rows = pl.ds(pl.multiple_of(i * half, 16), half)

            def chunk(d):
                return (src[rows, :] if d < 0 else ag[layer, d, rows, :]).astype(jnp.float32)

            total = jnp.zeros((half, 1), jnp.float32)
            for d in range(-1, n_head - 1):
                value = chunk(d)
                total = total + jnp.sum(value * value, axis=-1, keepdims=True)
            scale = lax.rsqrt(total / (feat * n_head) + 1e-05)
            for d in range(-1, n_head - 1):
                owner = lax.rem(me + n_head - 1 - d, n_head)
                value = chunk(d) * scale * gb[layer, 0:1, columns(owner)]
                normed[rows, columns(owner)] = value.astype(jnp.bfloat16)
            return carry

        lax.fori_loop(0, 2, norm_half, 0)
        if layer == 0:
            wq_local.wait()
            wq_fwd_in.wait_recv()

        def qkv_half(i, carry):
            rows = pl.ds(pl.multiple_of(i * half, 16), half)
            for slot in range(3):
                cols = slice(slot * feat, (slot + 1) * feat)
                value = jnp.dot(normed[rows, :], wq[layer, :, cols],
                                preferred_element_type=jnp.float32)
                if slot == 0:
                    value = value * (HEAD_DIM ** -0.5 * math.log2(math.e))
                if slot < 2:
                    qkv[rows, cols] = value.astype(jnp.bfloat16)
                else:
                    for h in range(heads):
                        vx[h, rows, :HEAD_DIM] = value[
                            :, h * HEAD_DIM:(h + 1) * HEAD_DIM].astype(jnp.bfloat16)
            return carry

        lax.fori_loop(0, 2, qkv_half, 0)
        if layer == 0:
            wo_in.wait_recv()
            wo_fwd.start()
            wo_local.wait()
            wo_fwd_in.wait_recv()

        def attend_half(i, carry):
            for sub, (offset, count) in enumerate(subs):
                rows = pl.ds(pl.multiple_of(i * half + offset, 16), count)
                for h in range(heads):
                    q = qkv[rows, h * HEAD_DIM:(h + 1) * HEAD_DIM]
                    k = qkv[:, feat + h * HEAD_DIM:feat + (h + 1) * HEAD_DIM]
                    scores = lax.dot_general(q, k, (((1,), (1,)), ((), ())),
                                             preferred_element_type=jnp.float32)
                    scores = jnp.where(lq_ref[layer, rows, :] == lk_ref[layer], scores, -1e30)
                    top = jnp.max(scores, axis=-1, keepdims=True)
                    expo = jnp.exp2(scores - top).astype(jnp.bfloat16)
                    both = jnp.dot(expo, vx[h], preferred_element_type=jnp.float32)
                    attb[rows, h * HEAD_DIM:(h + 1) * HEAD_DIM] = (
                        both[:, :HEAD_DIM] / both[:, HEAD_DIM:]).astype(jnp.bfloat16)
                block = attb[rows, :]
                for d in range(n_head - 1):
                    part[layer, d, rows, :] = jnp.dot(
                        block, wo[layer, :, columns(peers[d])],
                        preferred_element_type=jnp.float32).astype(jnp.bfloat16)
                    part_copy(layer, i * 2 + sub, rows, d).start()
                own[rows, :] = jnp.dot(block, wo[layer, :, columns(me)],
                                       preferred_element_type=jnp.float32)
            return carry

        lax.fori_loop(0, 2, attend_half, 0)

    def finish(layer, src, h, sub):
        offset, count = subs[sub]
        rows = pl.ds(h * half + offset, count)
        total = src[rows, :].astype(jnp.float32) + own[rows, :]
        for d in range(n_head - 1):
            part_copy(layer, h * 2 + sub, rows, d).wait_recv()
            total = total + parts_in[layer, d, rows, :].astype(jnp.float32)
        return rows, total.astype(jnp.bfloat16)

    wq_in.wait_recv()
    wq_fwd.start()
    gain_in.wait_recv()
    layer_compute(0, x_ref)

    low, high = pl.ds(0, half), pl.ds(half, half)
    rolls = []
    for sub, (offset, count) in enumerate(subs):
        rows, value = finish(0, x_ref, 0, sub)
        first_a[rows, :] = value
        roll = remote(first_a.at[rows], cur.at[pl.ds(half + offset, count)],
                      roll_send.at[sub], roll_recv.at[sub], {"win": left})
        roll.start()
        rolls.append(roll)
    for sub, (offset, count) in enumerate(subs):
        rows, value = finish(0, x_ref, 1, sub)
        cur[pl.ds(offset, count), :] = value
    gathers[1][0] = gather_copies(1, 0, cur)
    for c in gathers[1][0]:
        c.start()
    for roll in rolls:
        roll.wait_recv()
    gathers[1][1] = gather_copies(1, 1, cur)
    for c in gathers[1][1]:
        c.start()

    first_out = [
        remote(first_a, out_ref.at[seg, low], o_send.at[0], o_recv.at[0], there),
        remote(cur.at[low], out_ref.at[seg, high], o_send.at[1], o_recv.at[1], there),
    ]
    first_in = [
        remote(first_a, out_ref.at[other, low], o_send.at[0], o_recv.at[0], there),
        remote(cur.at[low], out_ref.at[other, high], o_send.at[1], o_recv.at[1], there),
    ]

    @pl.when(seg == 0)
    def _():
        out_ref[seg, low, :] = first_a[...]
        out_ref[seg, high, :] = cur[low, :]

    @pl.when(seg == 1)
    def _():
        for c in first_out:
            c.start()

    layer_compute(1, cur)

    second_sends, second_recvs = [], []
    for h in range(2):
        for sub in range(2):
            rows, value = finish(1, cur, h, sub)
            block = 2 + h * 2 + sub
            send = remote(second.at[rows], out_ref.at[seg, rows], o_send.at[block],
                          o_recv.at[block], there)
            second_sends.append(send)
            second_recvs.append(remote(second.at[rows], out_ref.at[other, rows],
                                       o_send.at[block], o_recv.at[block], there))
            second[rows, :] = value

            @pl.when(seg == 0)
            def _(send=send):
                send.start()

            @pl.when(seg == 1)
            def _(rows=rows, value=value):
                out_ref[seg, rows, :] = second[rows, :]

    for layer in range(2):
        for h in range(2):
            for c in gathers[layer][h]:
                c.wait_send()
            for sub, (offset, count) in enumerate(subs):
                rows = pl.ds(h * half + offset, count)
                for d in range(n_head - 1):
                    part_copy(layer, h * 2 + sub, rows, d).wait_send()
    for c in (gain_out, wq_out, wo_out, wq_fwd, wo_fwd, *rolls):
        c.wait_send()

    @pl.when(seg == 0)
    def _():
        for c in first_in:
            c.wait_recv()
        for c in second_sends:
            c.wait_send()

    @pl.when(seg == 1)
    def _():
        for c in first_out:
            c.wait_send()
        for c in second_recvs:
            c.wait_recv()


def to_halves(grid, half, fill):
    rows, cols, features = grid.shape
    split = grid.reshape(rows, 2, cols // 2, features).transpose(1, 0, 2, 3)
    split = split.reshape(2, rows * (cols // 2), features)
    split = jnp.pad(split, ((0, 0), (0, half - split.shape[1]), (0, 0)), constant_values=fill)
    return split.reshape(2 * half, features)


def body(n_head, n_win, inputs, gains, qkv_weight, out_weight, labels):
    seg = lax.axis_index("segment")
    micro, win_rows, win_cols, feat = inputs.shape
    cells = win_rows * (win_cols // 2)
    half = pad16(cells)
    tokens = 2 * half
    model = feat * n_head
    heads = feat // HEAD_DIM
    x = lax.dynamic_index_in_dim(inputs, seg, 0, keepdims=False)
    x = to_halves(x, half, 0)
    grid = labels[:, :, None]
    keys = jnp.stack([to_halves(jnp.zeros_like(grid), half, -1), to_halves(grid, half, -1)])
    queries = jnp.maximum(keys, 0)
    keys = keys.reshape(LAYERS, 1, tokens)
    gain_rows = jnp.broadcast_to(gains, (8, model))
    wq = qkv_weight[0].reshape(model, 3 * feat)
    wo = out_weight[0]
    bf16, f32 = jnp.bfloat16, jnp.float32
    others = n_head - 1
    dma = pltpu.SemaphoreType.DMA
    vmem = pl.BlockSpec(memory_space=pltpu.VMEM)
    hbm = pl.BlockSpec(memory_space=pl.ANY)
    out = pl.pallas_call(
        functools.partial(two_layers, n_head, n_win, half),
        out_shape=jax.ShapeDtypeStruct((micro, tokens, feat), bf16),
        in_specs=[vmem, vmem, vmem, vmem, hbm, hbm],
        out_specs=vmem,
        scratch_shapes=[
            pltpu.VMEM((LAYERS, model, 3 * feat), bf16),
            pltpu.VMEM((LAYERS, feat, model), bf16),
            pltpu.VMEM((LAYERS, 8, model), f32),
            pltpu.VMEM((LAYERS, others, tokens, feat), bf16),
            pltpu.VMEM((tokens, model), bf16),
            pltpu.VMEM((tokens, 2 * feat), bf16),
            pltpu.VMEM((heads, tokens, 2 * HEAD_DIM), bf16),
            pltpu.VMEM((tokens, feat), bf16),
            pltpu.VMEM((LAYERS, others, tokens, feat), bf16),
            pltpu.VMEM((LAYERS, others, tokens, feat), bf16),
            pltpu.VMEM((tokens, feat), f32),
            pltpu.VMEM((tokens, feat), bf16),
            pltpu.VMEM((half, feat), bf16),
            pltpu.VMEM((tokens, feat), bf16),
            dma((2,)), dma((3,)), dma((3,)), dma((2,)), dma((2,)),
            dma((LAYERS, 2, others)), dma((LAYERS, 2, others)),
            dma((LAYERS, 4, others)), dma((LAYERS, 4, others)),
            dma((2,)), dma((2,)), dma((6,)), dma((6,)),
        ],
        compiler_params=pltpu.CompilerParams(
            collective_id=0, has_side_effects=True, vmem_limit_bytes=58 * 2 ** 20),
    )(x, gain_rows, queries, keys, wq, wo)
    out = out.reshape(micro, 2, half, feat)[:, :, :cells]
    out = out.reshape(micro, 2, win_rows, win_cols // 2, feat).transpose(0, 2, 1, 3, 4)
    return out.reshape(1, micro, win_rows, win_cols, feat)


def solution(mesh):
    in_specs = (
        P(None, None, "win", "head"),
        P("segment", None),
        P("segment", None, None, "head"),
        P("segment", "head", None),
        P(None, "win"),
    )
    out_specs = P("segment", None, None, "win", "head")
    run = functools.partial(body, mesh.shape["head"], mesh.shape["win"])
    return jax.shard_map(run, mesh=mesh, in_specs=in_specs, out_specs=out_specs, check_vma=False)
```

time: 606 us -> 294 us (0.49)
  waiting for transfers between devices: 443 us -> 0 us
  Pallas kernels: 0 us -> 266 us
  matrix products: 79.5 us -> 0 us
  other arithmetic: 19 us -> 0.03 us
  starting transfers between devices: 17.2 us -> 0 us
  between operations: 13.4 us -> 0.09 us
  local copies, waits for them, and re-layouts: 31.2 us -> 23.6 us
    all_gather x6 -> x0, waiting for transfers between devices: 353 us -> none  [the longest x3 176 us: project(): lax.all_gather(grid_att, 'head', axis=2, tiled=True)]
    pallas_call x0 -> x1, Pallas kernels: none -> 266 us  [body(): pl.pallas_call(functools.partial(two_layers, n_head, n_win, half), out_sh...]
    ppermute x6 -> x0, waiting for transfers between devices: 62 us -> none  [the longest x3 46.9 us: shifted(): lax.ppermute(value, axis, [(source, source + steps) for source in range(f...]
    dot_general x9 -> x0, matrix products: 57.5 us -> none  [the longest x3 23.8 us: window_layer(): jnp.einsum('wtd,dcf->wtcf', win_normed, qkv_local, preferred_element_type...]
    all_to_all x1 -> x0, waiting for transfers between devices: 28.3 us -> none  [body(): lax.all_to_all(out_local, 'head', split_axis=1, concat_axis=0, tiled=True)]
    sub x3 -> x0, matrix products: 22 us -> none  [window_layer(): expo = jnp.exp(scores - top_score)]
    ppermute x6 -> x0, starting transfers between devices: 10.6 us -> none  [the longest x3 10.2 us: shifted(): lax.ppermute(value, axis, [(source, source + steps) for source in range(f...]
    convert_element_type x6 -> x0, local copies, waits for them, and re-layouts: 9.62 us -> none  [the longest x3 8.55 us: window_layer(): projected_qkv = jnp.einsum('wtd,dcf->wtcf', win_normed, qkv_local, prefer...]
  transfers between devices with their start and end apart: 13 -> 0, of which waited for: 13 -> 0; matrix products, arithmetic and copies ran while one was open for 1% -> 0% of each run, Pallas kernels for 0% -> 0%
where the time goes in v1:
time: 294 us; the launch traced here: 289 us
  Pallas kernels  266 us (90%)
  local copies, waits for them, and re-layouts  23.6 us (8%)
    pallas_call x1, Pallas kernels, body(): pl.pallas_call(functools.partial(two_layers, n_head, n_win, half), out_sh...  266 us
    unnamed x14, local copies, waits for them, and re-layouts  8.87 us

profile of v1, /device:TPU:0, one launch (start us, length us, event | category | flops | bytes accessed | tf_op | source)
XLA Modules:
  0.0 289.5 jit_solution(1977700211813842145)
XLA Ops:
  0.0 0.0 copy-start
  0.0 1.3 copy-done
  1.3 1.4 constant_dynamic-slice_fusion
  2.8 0.1 copy.29
  2.9 0.5 copy.20
  3.5 0.0 copy-start.2
  3.5 0.1 copy.31
  3.6 0.9 pad.13.clone
  4.5 0.0 copy-done.2
  4.5 0.1 copy.22
  4.6 0.1 copy.23
  4.7 0.1 reshape.72
  4.8 0.1 stack.8
  4.9 0.1 stack.7
  5.0 0.0 copy-start.1
  5.0 1.3 copy.25.lq_ref
  6.3 6.1 %copy.24 = bf16[1,1536,3,384]{1,3,2,0:T(8,128)(2,1)} copy(bf16[1,1536,3,384]{3,1,2,0:T(8,128)(2,1)} %param.7) | data formatting | bytes 7077888 | tf_op args[2]
  12.5 0.0 copy-done.1
  12.5 0.0 copy-start.3
  12.5 5.8 %copy.26.wq_hbm = bf16[1536,1152]{1,0:T(8,128)(2,1)} copy(bf16[1536,1152]{0,1:T(8,128)(2,1)} %bitcast.20) | data formatting | bytes 7077888 | tf_op jit(solution)/shard_map/reshape;squeeze | solution.py:310
  18.3 0.0 copy-done.3
  18.3 0.6 broadcast_in_dim.8.gain_ref
  19.0 265.8 %shard_map.55 = bf16[2,928,384]{2,1,0:T(8,128)(2,1)} custom-call(bf16[928,384]{1,0:T(8,128)(2,1)} %bitcast.24, f32[8,1536]{1,0:T(8,128)} %broadcast_in_dim.8.gain_ref, s32[2,928,1]{2,1,0:T(8,128)} %copy.25.lq_ref, s32[2,1,928]{2,1,0:T(1,128)} %bitcast.28, bf16[1536,1152]{1,0:T(8,128)(2,1)} %copy.26.wq_hbm, bf16[384,1536]{1,0:T(8,128)(2,1)} %bitcast.26), custom_call_target="tpu_custom_call" | custom-call | tf_op jit(solution)/shard_map/pallas_call | solution.py:317
  284.8 1.5 slice.4
  286.3 1.1 copy.30
  287.3 2.1 copy.28
  (9 shorter events, 0.1 us)
Async XLA Ops:
  0.0 1.3 copy-start
  3.5 1.0 copy-start.2
  5.0 7.4 %copy-start.1 = (s32[2,928,1]{1,2,0:T(1,128)}, s32[2,928,1]{1,2,0:T(1,128)S(1)}, u32[]{:S(2)}) copy-start(s32[2,928,1]{1,2,0:T(1,128)S(1)} %constant_dynamic-update-slice_fusion) | copy-start | bytes 22276
  12.5 5.8 %copy-start.3 = (f32[1,1536]{1,0:T(1,128)S(1)}, f32[1,1536]{1,0:T(1,128)}, u32[]{:S(2)}) copy-start(f32[1,1536]{1,0:T(1,128)} %param.6) | copy-start | bytes 18436

commit v2 on v1

v2 whole, which is shorter than its diff:
```python
import functools
import math

import jax
import jax.numpy as jnp
from jax import lax
from jax.experimental import pallas as pl
from jax.experimental.pallas import tpu as pltpu
from jax.sharding import PartitionSpec as P

HEAD_DIM = 128
WIN_SIDE = 30
MESH = pl.DeviceIdType.MESH
LAYERS = 2


def pad16(n):
    return -(-n // 16) * 16


def remote(src, dst, send, recv, device):
    return pltpu.make_async_remote_copy(
        src_ref=src, dst_ref=dst, send_sem=send, recv_sem=recv,
        device_id=device, device_id_type=MESH,
    )


def two_layers(
    n_head, n_win, half,
    x_ref, gain_ref, lq_ref, lk_ref, wq_hbm, wo_hbm,
    out_ref,
    wq, wo, gb, ag, normed, qkv, vx, attb, part, sums, sums_in, cur, first_a, second,
    loc_sem, wsend, wrecv, fsend, frecv, ag_send, ag_recv, rs_send, rs_recv,
    roll_send, roll_recv, o_send, o_recv,
):
    seg = lax.axis_index("segment")
    win = lax.axis_index("win")
    me = lax.axis_index("head")
    last = n_head - 1
    other = 1 - seg
    core = lax.rem(win, 2)
    mate = win + 1 - 2 * core
    left = lax.rem(win + n_win - 1, n_win)
    right = lax.rem(win + 1, n_win)
    tokens, feat = x_ref.shape
    heads = feat // HEAD_DIM
    first_rows = pad16(half // 2)
    blocks = ((0, first_rows), (first_rows, half - first_rows),
              (half, first_rows), (half + first_rows, half - first_rows))
    up, down = {"head": me + 1}, {"head": me - 1}
    there, beside = {"segment": other}, {"win": mate}

    wq_local = pltpu.make_async_copy(wq_hbm, wq.at[seg], loc_sem.at[0])
    wo_local = pltpu.make_async_copy(wo_hbm, wo.at[seg], loc_sem.at[1])
    wq_local.start()
    wo_local.start()

    barrier = pltpu.get_barrier_semaphore()

    @pl.when(me < last)
    def _():
        pl.semaphore_signal(barrier, inc=1, device_id=up, device_id_type=MESH)

    @pl.when(me > 0)
    def _():
        pl.semaphore_signal(barrier, inc=1, device_id=down, device_id_type=MESH)

    pl.semaphore_signal(barrier, inc=1, device_id=there, device_id_type=MESH)
    for w in (mate, left, right):
        pl.semaphore_signal(barrier, inc=1, device_id={"win": w}, device_id_type=MESH)

    @pl.when((me > 0) & (me < last))
    def _():
        pl.semaphore_wait(barrier, 6)

    @pl.when((me == 0) | (me == last))
    def _():
        pl.semaphore_wait(barrier, 5)

    def rows_of(block):
        return pl.ds(blocks[block][0], blocks[block][1])

    def ag_copy(layer, way, hop, block, owner, src):
        rows = rows_of(block)
        source = ag.at[layer, owner, rows] if src is None else src.at[rows]
        return remote(source, ag.at[layer, owner, rows], ag_send.at[layer, way, hop, block],
                      ag_recv.at[layer, way, hop, block], up if way == 0 else down)

    def gather_start(layer, src, block):
        @pl.when(me < last)
        def _():
            ag_copy(layer, 0, 0, block, me, src).start()

        @pl.when(me > 0)
        def _():
            ag_copy(layer, 1, 0, block, me, src).start()

    def gather_step(layer, hop, block):
        behind, ahead = me - 1 - hop, me + 1 + hop

        @pl.when(behind >= 0)
        def _():
            ag_copy(layer, 0, hop, block, behind, None).wait_recv()
            if hop + 1 < last:
                @pl.when(me < last)
                def _():
                    ag_copy(layer, 0, hop + 1, block, behind, None).start()

        @pl.when(ahead <= last)
        def _():
            ag_copy(layer, 1, hop, block, ahead, None).wait_recv()
            if hop + 1 < last:
                @pl.when(me > 0)
                def _():
                    ag_copy(layer, 1, hop + 1, block, ahead, None).start()

    def gather_sent(layer, src, block):
        for hop in range(last):
            @pl.when((me - hop >= 0) & (me < last))
            def _(hop=hop):
                ag_copy(layer, 0, hop, block, me - hop, None if hop else src).wait_send()

            @pl.when((me + hop <= last) & (me > 0))
            def _(hop=hop):
                ag_copy(layer, 1, hop, block, me + hop, None if hop else src).wait_send()

    def sum_copy(layer, way, block, rows, owner):
        return remote(sums.at[layer, owner, rows], sums_in.at[layer, way, owner, rows],
                      rs_send.at[layer, way, block, owner], rs_recv.at[layer, way, block, owner],
                      up if way == 0 else down)

    q_rows, o_rows = wq_hbm.shape[1] // 2, wo_hbm.shape[0] // 2
    mine_q = pl.ds(pl.multiple_of(core * q_rows, 16), q_rows)
    mine_o = pl.ds(pl.multiple_of(core * o_rows, 16), o_rows)
    mate_q = pl.ds(pl.multiple_of((1 - core) * q_rows, 16), q_rows)
    mate_o = pl.ds(pl.multiple_of((1 - core) * o_rows, 16), o_rows)
    every = pl.ds(0, 3)

    for block in range(4):
        gather_start(0, x_ref, block)
    gain_out = remote(gain_ref, gb.at[seg], wsend.at[2], wrecv.at[2], there)
    wq_out = remote(wq_hbm.at[every, mine_q], wq.at[seg, every, mine_q],
                    wsend.at[0], wrecv.at[0], there)
    wo_out = remote(wo_hbm.at[mine_o], wo.at[seg, mine_o], wsend.at[1], wrecv.at[1], there)
    gain_out.start()
    wq_out.start()
    wo_out.start()
    gb[seg] = gain_ref[...]
    for h in range(heads):
        vx[h, :, HEAD_DIM:] = jnp.ones((tokens, HEAD_DIM), jnp.bfloat16)

    wq_theirs, wq_mates = wq.at[other, every, mine_q], wq.at[other, every, mate_q]
    wq_in = remote(wq_hbm.at[every, mine_q], wq_theirs, wsend.at[0], wrecv.at[0], there)
    wo_in = remote(wo_hbm.at[mine_o], wo.at[other, mine_o], wsend.at[1], wrecv.at[1], there)
    gain_in = remote(gain_ref, gb.at[other], wsend.at[2], wrecv.at[2], there)
    wq_fwd = remote(wq_theirs, wq_theirs, fsend.at[0], frecv.at[0], beside)
    wo_fwd = remote(wo.at[other, mine_o], wo.at[other, mine_o], fsend.at[1], frecv.at[1], beside)
    wq_fwd_in = remote(wq_mates, wq_mates, fsend.at[0], frecv.at[0], beside)
    wo_fwd_in = remote(wo.at[other, mate_o], wo.at[other, mate_o], fsend.at[1], frecv.at[1], beside)

    def columns(owner):
        return pl.ds(pl.multiple_of(owner * feat, 128), feat)

    def layer_compute(layer, src):
        ag[layer, me] = src[...]

        def norm_half(i, carry):
            rows = pl.ds(pl.multiple_of(i * half, 16), half)
            total = jnp.zeros((half, 1), jnp.float32)
            for owner in range(n_head):
                value = ag[layer, owner, rows, :].astype(jnp.float32)
                total = total + jnp.sum(value * value, axis=-1, keepdims=True)
            scale = lax.rsqrt(total / (feat * n_head) + 1e-05)
            for owner in range(n_head):
                cols = slice(owner * feat, (owner + 1) * feat)
                value = ag[layer, owner, rows, :].astype(jnp.float32)
                normed[rows, cols] = (value * scale * gb[layer, 0:1, cols]).astype(jnp.bfloat16)
            return carry

        lax.fori_loop(0, 2, norm_half, 0)
        if layer == 0:
            wq_local.wait()
            wq_fwd_in.wait_recv()

        def qkv_half(i, carry):
            rows = pl.ds(pl.multiple_of(i * half, 16), half)
            for slot in range(3):
                value = jnp.dot(normed[rows, :], wq[layer, slot],
                                preferred_element_type=jnp.float32)
                if slot == 0:
                    value = value * (HEAD_DIM ** -0.5 * math.log2(math.e))
                if slot < 2:
                    qkv[rows, slot * feat:(slot + 1) * feat] = value.astype(jnp.bfloat16)
                else:
                    for h in range(heads):
                        vx[h, rows, :HEAD_DIM] = value[
                            :, h * HEAD_DIM:(h + 1) * HEAD_DIM].astype(jnp.bfloat16)
            return carry

        lax.fori_loop(0, 2, qkv_half, 0)
        if layer == 0:
            wo_in.wait_recv()
            wo_fwd.start()
            wo_local.wait()
            wo_fwd_in.wait_recv()

        def attend_half(i, carry):
            for sub in range(2):
                offset, count = blocks[sub]
                rows = pl.ds(pl.multiple_of(i * half + offset, 16), count)
                for h in range(heads):
                    q = qkv[rows, h * HEAD_DIM:(h + 1) * HEAD_DIM]
                    k = qkv[:, feat + h * HEAD_DIM:feat + (h + 1) * HEAD_DIM]
                    scores = lax.dot_general(q, k, (((1,), (1,)), ((), ())),
                                             preferred_element_type=jnp.float32)
                    scores = jnp.where(lq_ref[layer, rows, :] == lk_ref[layer], scores, -1e30)
                    top = jnp.max(scores, axis=-1, keepdims=True)
                    expo = jnp.exp2(scores - top).astype(jnp.bfloat16)
                    both = jnp.dot(expo, vx[h], preferred_element_type=jnp.float32)
                    attb[rows, h * HEAD_DIM:(h + 1) * HEAD_DIM] = (
                        both[:, :HEAD_DIM] / both[:, HEAD_DIM:]).astype(jnp.bfloat16)
                block = attb[rows, :]
                for owner in range(n_head):
                    part[owner, rows, :] = jnp.dot(
                        block, wo[layer, :, owner * feat:(owner + 1) * feat],
                        preferred_element_type=jnp.float32)

                @pl.when(me == 0)
                def _(rows=rows, sub=sub):
                    for owner in range(last, 0, -1):
                        sums[layer, owner, rows, :] = part[owner, rows, :].astype(jnp.bfloat16)
                        sum_copy(layer, 0, i * 2 + sub, rows, owner).start()

                @pl.when(me == last)
                def _(rows=rows, sub=sub):
                    for owner in range(last):
                        sums[layer, owner, rows, :] = part[owner, rows, :].astype(jnp.bfloat16)
                        sum_copy(layer, 1, i * 2 + sub, rows, owner).start()
            return carry

        lax.fori_loop(0, 2, attend_half, 0)

    def finish(layer, src, block):
        rows = rows_of(block)
        for far in range(last - 1, -1, -1):
            for way, owner, takes in ((0, me + far, me > 0), (1, me - far, me < last)):
                @pl.when(takes & (owner >= 0) & (owner <= last))
                def _(way=way, owner=owner, far=far):
                    copy = sum_copy(layer, way, block, rows, owner)
                    copy.wait_recv()
                    total = part[owner, rows, :] + sums_in[
                        layer, way, owner, rows, :].astype(jnp.float32)
                    if far:
                        sums[layer, owner, rows, :] = total.astype(jnp.bfloat16)
                        copy.start()
                    else:
                        part[owner, rows, :] = total
        total = src[rows, :].astype(jnp.float32) + part[me, rows, :]
        return rows, total.astype(jnp.bfloat16)

    def sums_sent(layer, block):
        for far in range(1, n_head):
            for way, owner in ((0, me + far), (1, me - far)):
                @pl.when((owner >= 0) & (owner <= last))
                def _(way=way, owner=owner):
                    sum_copy(layer, way, block, rows_of(block), owner).wait_send()

    for hop in range(last - 1):
        for block in range(4):
            gather_step(0, hop, block)
    wq_in.wait_recv()
    wq_fwd.start()
    gain_in.wait_recv()
    for block in range(4):
        gather_step(0, last - 1, block)
    layer_compute(0, x_ref)

    low, high = pl.ds(0, half), pl.ds(half, half)
    rolls = []
    for block in range(2):
        rows, value = finish(0, x_ref, block)
        first_a[rows, :] = value
        roll = remote(first_a.at[rows], cur.at[rows_of(2 + block)],
                      roll_send.at[block], roll_recv.at[block], {"win": left})
        roll.start()
        rolls.append(roll)
    for block in range(2):
        rolls[block].wait_recv()
        gather_start(1, cur, 2 + block)
    for block in range(2):
        _, value = finish(0, x_ref, 2 + block)
        cur[rows_of(block), :] = value
        gather_start(1, cur, block)
        if block < last - 1:
            for late in (2, 3):
                gather_step(1, block, late)
    for late in (2, 3):
        for hop in range(min(2, last - 1), last):
            gather_step(1, hop, late)
    for hop in range(last):
        for block in range(2):
            gather_step(1, hop, block)

    first_out = [
        remote(first_a, out_ref.at[seg, low], o_send.at[0], o_recv.at[0], there),
        remote(cur.at[low], out_ref.at[seg, high], o_send.at[1], o_recv.at[1], there),
    ]
    first_in = [
        remote(first_a, out_ref.at[other, low], o_send.at[0], o_recv.at[0], there),
        remote(cur.at[low], out_ref.at[other, high], o_send.at[1], o_recv.at[1], there),
    ]

    @pl.when(seg == 0)
    def _():
        out_ref[seg, low, :] = first_a[...]
        out_ref[seg, high, :] = cur[low, :]

    @pl.when(seg == 1)
    def _():
        for c in first_out:
            c.start()

    layer_compute(1, cur)

    second_sends, second_recvs = [], []
    for block in range(4):
        rows, value = finish(1, cur, block)
        send = remote(second.at[rows], out_ref.at[seg, rows], o_send.at[2 + block],
                      o_recv.at[2 + block], there)
        second_sends.append(send)
        second_recvs.append(remote(second.at[rows], out_ref.at[other, rows],
                                   o_send.at[2 + block], o_recv.at[2 + block], there))
        second[rows, :] = value

        @pl.when(seg == 0)
        def _(send=send):
            send.start()

        @pl.when(seg == 1)
        def _(rows=rows):
            out_ref[seg, rows, :] = second[rows, :]

    for layer, src in ((0, x_ref), (1, cur)):
        for block in range(4):
            gather_sent(layer, src, block)
            sums_sent(layer, block)
    for c in (gain_out, wq_out, wo_out, wq_fwd, wo_fwd, *rolls):
        c.wait_send()

    @pl.when(seg == 0)
    def _():
        for c in first_in:
            c.wait_recv()
        for c in second_sends:
            c.wait_send()

    @pl.when(seg == 1)
    def _():
        for c in first_out:
            c.wait_send()
        for c in second_recvs:
            c.wait_recv()


def to_halves(grid, half, fill):
    rows, cols, features = grid.shape
    split = grid.reshape(rows, 2, cols // 2, features).transpose(1, 0, 2, 3)
    split = split.reshape(2, rows * (cols // 2), features)
    split = jnp.pad(split, ((0, 0), (0, half - split.shape[1]), (0, 0)), constant_values=fill)
    return split.reshape(2 * half, features)


def body(n_head, n_win, inputs, gains, qkv_weight, out_weight, labels):
    seg = lax.axis_index("segment")
    micro, win_rows, win_cols, feat = inputs.shape
    cells = win_rows * (win_cols // 2)
    half = pad16(cells)
    tokens = 2 * half
    model = feat * n_head
    heads = feat // HEAD_DIM
    x = lax.dynamic_index_in_dim(inputs, seg, 0, keepdims=False)
    x = to_halves(x, half, 0)
    grid = labels[:, :, None]
    keys = jnp.stack([to_halves(jnp.zeros_like(grid), half, -1), to_halves(grid, half, -1)])
    queries = jnp.maximum(keys, 0)
    keys = keys.reshape(LAYERS, 1, tokens)
    gain_rows = jnp.broadcast_to(gains, (8, model))
    wq = qkv_weight[0].transpose(1, 0, 2)
    wo = out_weight[0]
    bf16, f32 = jnp.bfloat16, jnp.float32
    others = n_head - 1
    dma = pltpu.SemaphoreType.DMA
    vmem = pl.BlockSpec(memory_space=pltpu.VMEM)
    hbm = pl.BlockSpec(memory_space=pl.ANY)
    out = pl.pallas_call(
        functools.partial(two_layers, n_head, n_win, half),
        out_shape=jax.ShapeDtypeStruct((micro, tokens, feat), bf16),
        in_specs=[vmem, vmem, vmem, vmem, hbm, hbm],
        out_specs=vmem,
        scratch_shapes=[
            pltpu.VMEM((LAYERS, 3, model, feat), bf16),
            pltpu.VMEM((LAYERS, feat, model), bf16),
            pltpu.VMEM((LAYERS, 8, model), f32),
            pltpu.VMEM((LAYERS, n_head, tokens, feat), bf16),
            pltpu.VMEM((tokens, model), bf16),
            pltpu.VMEM((tokens, 2 * feat), bf16),
            pltpu.VMEM((heads, tokens, 2 * HEAD_DIM), bf16),
            pltpu.VMEM((tokens, feat), bf16),
            pltpu.VMEM((n_head, tokens, feat), f32),
            pltpu.VMEM((LAYERS, n_head, tokens, feat), bf16),
            pltpu.VMEM((LAYERS, 2, n_head, tokens, feat), bf16),
            pltpu.VMEM((tokens, feat), bf16),
            pltpu.VMEM((half, feat), bf16),
            pltpu.VMEM((tokens, feat), bf16),
            dma((2,)), dma((3,)), dma((3,)), dma((2,)), dma((2,)),
            dma((LAYERS, 2, others, 4)), dma((LAYERS, 2, others, 4)),
            dma((LAYERS, 2, 4, n_head)), dma((LAYERS, 2, 4, n_head)),
            dma((2,)), dma((2,)), dma((6,)), dma((6,)),
        ],
        compiler_params=pltpu.CompilerParams(
            collective_id=0, has_side_effects=True, vmem_limit_bytes=58 * 2 ** 20),
    )(x, gain_rows, queries, keys, wq, wo)
    out = out.reshape(micro, 2, half, feat)[:, :, :cells]
    out = out.reshape(micro, 2, win_rows, win_cols // 2, feat).transpose(0, 2, 1, 3, 4)
    return out.reshape(1, micro, win_rows, win_cols, feat)


def solution(mesh):
    in_specs = (
        P(None, None, "win", "head"),
        P("segment", None),
        P("segment", None, None, "head"),
        P("segment", "head", None),
        P(None, "win"),
    )
    out_specs = P("segment", None, None, "win", "head")
    run = functools.partial(body, mesh.shape["head"], mesh.shape["win"])
    return jax.shard_map(run, mesh=mesh, in_specs=in_specs, out_specs=out_specs, check_vma=False)
```

time: 294 us -> 239 us (0.81); the launches traced: 289 us -> 238 us
  Pallas kernels: 266 us -> 226 us
  local copies, waits for them, and re-layouts: 23.6 us -> 11 us
    pallas_call x1, Pallas kernels: 266 us -> 226 us  [body(): pl.pallas_call(functools.partial(two_layers, n_head, n_win, half), out_sh...]
    unnamed x14 -> x9, local copies, waits for them, and re-layouts: 8.87 us -> 2.11 us
    another operation x1 -> x0, local copies, waits for them, and re-layouts: 5.84 us -> none  [body(): wq = qkv_weight[0].reshape(model, 3 * feat)]
where the time goes in v2:
time: 239 us; the launch traced here: 238 us
  Pallas kernels  226 us (95%)
  local copies, waits for them, and re-layouts  11 us (5%)
    pallas_call x1, Pallas kernels, body(): pl.pallas_call(functools.partial(two_layers, n_head, n_win, half), out_sh...  226 us

profile of v2, /device:TPU:0, one launch (start us, length us, event | category | flops | bytes accessed | tf_op | source)
XLA Modules:
  0.0 237.6 jit_solution(4439379865102044514)
XLA Ops:
  0.0 0.0 copy-start
  0.0 0.1 stack.7
  0.1 0.8 reduce
  0.9 0.8 copy.19
  1.7 0.1 copy.20
  1.8 0.1 reshape.72
  2.0 0.1 stack.8
  2.1 0.0 copy-start.1
  2.1 0.6 broadcast_in_dim.8.gain_ref
  2.7 1.3 copy.21.lq_ref
  4.0 0.0 copy-done
  4.0 1.4 constant_dynamic-slice_fusion
  5.4 0.0 copy-done.1
  5.4 0.1 copy.24
  5.6 0.5 copy.17
  6.1 0.1 copy.26
  6.2 0.9 pad.13.clone
  7.1 225.7 %shard_map.55 = bf16[2,928,384]{2,1,0:T(8,128)(2,1)} custom-call(bf16[928,384]{1,0:T(8,128)(2,1)} %bitcast.26, f32[8,1536]{1,0:T(8,128)} %broadcast_in_dim.8.gain_ref, s32[2,928,1]{2,1,0:T(8,128)} %copy.21.lq_ref, s32[2,1,928]{2,1,0:T(1,128)} %bitcast.30, bf16[3,1536,384]{2,1,0:T(8,128)(2,1)} %bitcast.24, bf16[384,1536]{1,0:T(8,128)(2,1)} %bitcast.28), custom_call_target="tpu_custom_call" | custom-call | tf_op jit(solution)/shard_map/pallas_call | solution.py:395
  232.9 1.5 slice.4
  234.4 1.1 copy.25
  235.5 2.1 copy.23
  (8 shorter events, 0.1 us)
Async XLA Ops:
  0.0 4.0 %copy-start = (bf16[2,30,30,384]{3,0,2,1:T(2,128)(2,1)S(1)}, bf16[2,30,30,384]{3,0,2,1:T(2,128)(2,1)}, u32[]{:S(2)}) copy-start(bf16[2,30,30,384]{3,0,2,1:T(2,128)(2,1)} %param.5) | copy-start | bytes 4147204
  2.1 3.4 %copy-start.1 = (s32[2,928,1]{1,2,0:T(1,128)}, s32[2,928,1]{1,2,0:T(1,128)S(1)}, u32[]{:S(2)}) copy-start(s32[2,928,1]{1,2,0:T(1,128)S(1)} %constant_dynamic-update-slice_fusion) | copy-start | bytes 22276

commit v3 on v2

--- a/solution.py
+++ b/solution.py
@@ -144,7 +144,6 @@
     wo_out = remote(wo_hbm.at[mine_o], wo.at[seg, mine_o], wsend.at[1], wrecv.at[1], there)
     gain_out.start()
     wq_out.start()
-    wo_out.start()
     gb[seg] = gain_ref[...]
     for h in range(heads):
         vx[h, :, HEAD_DIM:] = jnp.ones((tokens, HEAD_DIM), jnp.bfloat16)
@@ -161,11 +160,10 @@
     def columns(owner):
         return pl.ds(pl.multiple_of(owner * feat, 128), feat)
 
-    def layer_compute(layer, src):
-        ag[layer, me] = src[...]
-
+    def prepare(layer, src, begin, end):
         def norm_half(i, carry):
             rows = pl.ds(pl.multiple_of(i * half, 16), half)
+            ag[layer, me, rows, :] = src[rows, :]
             total = jnp.zeros((half, 1), jnp.float32)
             for owner in range(n_head):
                 value = ag[layer, owner, rows, :].astype(jnp.float32)
@@ -177,7 +175,7 @@
                 normed[rows, cols] = (value * scale * gb[layer, 0:1, cols]).astype(jnp.bfloat16)
             return carry
 
-        lax.fori_loop(0, 2, norm_half, 0)
+        lax.fori_loop(begin, end, norm_half, 0)
         if layer == 0:
             wq_local.wait()
             wq_fwd_in.wait_recv()
@@ -197,7 +195,9 @@
                             :, h * HEAD_DIM:(h + 1) * HEAD_DIM].astype(jnp.bfloat16)
             return carry
 
-        lax.fori_loop(0, 2, qkv_half, 0)
+        lax.fori_loop(begin, end, qkv_half, 0)
+
+    def attend(layer):
         if layer == 0:
             wo_in.wait_recv()
             wo_fwd.start()
@@ -270,10 +270,12 @@
             gather_step(0, hop, block)
     wq_in.wait_recv()
     wq_fwd.start()
+    wo_out.start()
     gain_in.wait_recv()
     for block in range(4):
         gather_step(0, last - 1, block)
-    layer_compute(0, x_ref)
+    prepare(0, x_ref, 0, 2)
+    attend(0)
 
     low, high = pl.ds(0, half), pl.ds(half, half)
     rolls = []
@@ -300,6 +302,9 @@
     for hop in range(last):
         for block in range(2):
             gather_step(1, hop, block)
+        if hop == 0:
+            prepare(1, cur, 1, 2)
+    prepare(1, cur, 0, 1)
 
     first_out = [
         remote(first_a, out_ref.at[seg, low], o_send.at[0], o_recv.at[0], there),
@@ -320,7 +325,7 @@
         for c in first_out:
             c.start()
 
-    layer_compute(1, cur)
+    attend(1)
 
     second_sends, second_recvs = [], []
     for block in range(4):

time: 239 us -> 235 us (0.983)
  Pallas kernels: 226 us -> 223 us
    pallas_call x1, Pallas kernels: 226 us -> 223 us  [body(): pl.pallas_call(functools.partial(two_layers, n_head, n_win, half), out_sh...]
where the time goes in v3:
time: 235 us; the launch traced here: 234 us
  Pallas kernels  223 us (95%)
  local copies, waits for them, and re-layouts  11 us (5%)
    pallas_call x1, Pallas kernels, body(): pl.pallas_call(functools.partial(two_layers, n_head, n_win, half), out_sh...  223 us

profile of v3, /device:TPU:0, one launch (start us, length us, event | category | flops | bytes accessed | tf_op | source)
XLA Modules:
  0.0 234.4 jit_solution(13327019567014998231)
XLA Ops:
  0.0 0.0 copy-start
  0.0 0.1 stack.7
  0.1 0.8 reduce
  0.9 0.8 copy.19
  1.7 0.1 copy.20
  1.8 0.1 reshape.72
  2.0 0.1 stack.8
  2.1 0.0 copy-start.1
  2.1 0.6 broadcast_in_dim.8.gain_ref
  2.7 1.3 copy.21.lq_ref
  4.0 0.0 copy-done
  4.0 1.4 constant_dynamic-slice_fusion
  5.4 0.0 copy-done.1
  5.4 0.1 copy.24
  5.6 0.5 copy.17
  6.1 0.1 copy.26
  6.2 0.9 pad.13.clone
  7.1 222.5 %shard_map.55 = bf16[2,928,384]{2,1,0:T(8,128)(2,1)} custom-call(bf16[928,384]{1,0:T(8,128)(2,1)} %bitcast.26, f32[8,1536]{1,0:T(8,128)} %broadcast_in_dim.8.gain_ref, s32[2,928,1]{2,1,0:T(8,128)} %copy.21.lq_ref, s32[2,1,928]{2,1,0:T(1,128)} %bitcast.30, bf16[3,1536,384]{2,1,0:T(8,128)(2,1)} %bitcast.24, bf16[384,1536]{1,0:T(8,128)(2,1)} %bitcast.28), custom_call_target="tpu_custom_call" | custom-call | tf_op jit(solution)/shard_map/pallas_call | solution.py:400
  229.7 1.5 slice.4
  231.2 1.1 copy.25
  232.3 2.1 copy.23
  (8 shorter events, 0.1 us)
Async XLA Ops:
  0.0 4.0 %copy-start = (bf16[2,30,30,384]{3,0,2,1:T(2,128)(2,1)S(1)}, bf16[2,30,30,384]{3,0,2,1:T(2,128)(2,1)}, u32[]{:S(2)}) copy-start(bf16[2,30,30,384]{3,0,2,1:T(2,128)(2,1)} %param.5) | copy-start | bytes 4147204
  2.1 3.4 %copy-start.1 = (s32[2,928,1]{1,2,0:T(1,128)}, s32[2,928,1]{1,2,0:T(1,128)S(1)}, u32[]{:S(2)}) copy-start(s32[2,928,1]{1,2,0:T(1,128)S(1)} %constant_dynamic-update-slice_fusion) | copy-start | bytes 22276
